TPU v7x, 512 devices: a whole 4x8x8 slice. The times are simulated.
512 devices in a mesh: ctx: 64 (over z, y), head: 8 (over x, core).
Axes of the slice: x: 4, y: 8, z: 8, core: 2. Of those that a mesh axis runs over, the one named last changes fastest.
Arguments:
- queries: bfloat16 [512, 8192], P('ctx', 'head'), may hold values from -6 to 6
- cache_keys: bfloat16 [65536, 8, 128], P('ctx', 'head'), may hold values from -6 to 6
- cache_values: bfloat16 [65536, 8, 128], P('ctx', 'head'), may hold values from -6 to 6
- vertical_blocks: int32 [64, 8], P('head'), may hold values from 0 to 511, as said below
- slash_offsets: int32 [64, 48], P('head'), may hold values from 0 to 511, as said below
- out_weight: bfloat16 [8192, 8192], P('head', 'ctx'), may hold values from -0.0625 to 0.0625
Outputs:
- projected: bfloat16 [512, 8192], P('head', 'ctx')
Inputs may be any that keep to these rules, and one draw needn't show every extreme that they name: `vertical_blocks`: every head's list holds block 0; entries may repeat, and a block counts once however often it is named. `slash_offsets`: every head's list holds offset 0; entries may repeat, and a block counts once however often it is reached.
All inputs are finite; a program needn't handle non-finite values.
Results may differ from a plain program's by a relative error of at most 0.007.
Values may be sent and summed in bfloat16 or wider, within the bound.
A program may use at most 64 MiB of HBM per device.

v0:
```python
from functools import partial

import jax
import jax.numpy as jnp
from jax import lax
from jax.sharding import PartitionSpec as P

BLOCK = 128


NEG_FILL = -1e30


def block_terms(q_four, key_block, value_block, allowed_mask, score_scale):
    kv_local = q_four.shape[1]
    group_size = q_four.shape[2]
    scores = (
        jnp.einsum("qgjd,kgd->qgjk", q_four, key_block, preferred_element_type=jnp.float32)
        * score_scale
    )
    scores = scores.reshape(scores.shape[0], kv_local * group_size, scores.shape[3])
    masked = jnp.where(allowed_mask, scores, NEG_FILL)
    block_peak = jnp.max(masked, axis=-1)
    safe_peak = jnp.where(block_peak > 0.5 * NEG_FILL, block_peak, 0.0)
    weights = jnp.where(allowed_mask, jnp.exp(scores - safe_peak[..., None]), 0.0).astype(
        jnp.bfloat16
    )
    block_total = jnp.sum(weights.astype(jnp.float32), axis=-1)
    weights_four = weights.reshape(weights.shape[0], kv_local, group_size, weights.shape[2])
    block_out = jnp.einsum(
        "qgjk,kgd->qgjd", weights_four, value_block, preferred_element_type=jnp.float32
    )
    return (
        block_peak,
        block_total,
        block_out.reshape(block_out.shape[0], kv_local * group_size, block_out.shape[3]),
    )


def body(queries, cache_keys, cache_values, vertical_blocks, slash_offsets, out_weight):
    ctx_count = lax.axis_size("ctx")
    ctx_place = lax.axis_index("ctx")
    q_whole = lax.all_gather(queries, "ctx", axis=0, tiled=True)
    q_total = q_whole.shape[0]
    local_len, kv_local, head_width = cache_keys.shape
    heads_local = vertical_blocks.shape[0]
    group_size = heads_local // kv_local
    local_blocks = local_len // BLOCK
    q_blocks = q_total // BLOCK
    all_blocks = local_blocks * ctx_count
    score_scale = float(head_width) ** (-0.5)
    q_four = q_whole.reshape(q_total, kv_local, group_size, head_width)
    block_ids = ctx_place * local_blocks + jnp.arange(local_blocks, dtype=jnp.int32)
    query_blocks = all_blocks - q_blocks + jnp.arange(q_blocks, dtype=jnp.int32)
    vertical_hit = jnp.any(vertical_blocks[:, :, None] == block_ids[None, None, :], axis=1)
    offsets = query_blocks[:, None] - block_ids[None, :]
    slash_hit = jnp.any(slash_offsets[:, None, None, :] == offsets[None, :, :, None], axis=3)
    chosen = jnp.transpose(vertical_hit[:, None, :] | slash_hit, (1, 0, 2))
    first_query = all_blocks * BLOCK - q_total
    query_pos = first_query + jnp.arange(q_total, dtype=jnp.int32)

    def visit_block(turn_index, state_carry, block_order):
        run_peak, run_total, run_out = state_carry
        local_block = block_order[turn_index]
        key_block = lax.dynamic_slice_in_dim(cache_keys, local_block * BLOCK, BLOCK, 0)
        value_block = lax.dynamic_slice_in_dim(cache_values, local_block * BLOCK, BLOCK, 0)
        picked = lax.dynamic_index_in_dim(chosen, local_block, 2, keepdims=False)
        picked_rows = jnp.repeat(picked, BLOCK, axis=0)
        key_pos = ctx_place * local_len + local_block * BLOCK + jnp.arange(BLOCK, dtype=jnp.int32)
        allowed_mask = picked_rows[:, :, None] & (
            key_pos[None, None, :] <= query_pos[:, None, None]
        )
        block_peak, block_total, block_out = block_terms(
            q_four, key_block, value_block, allowed_mask, score_scale
        )
        new_peak = jnp.maximum(run_peak, block_peak)
        old_factor = jnp.exp(run_peak - new_peak)
        new_factor = jnp.exp(block_peak - new_peak)
        new_total = run_total * old_factor + block_total * new_factor
        new_out = run_out * old_factor[..., None] + block_out * new_factor[..., None]
        return (new_peak, new_total, new_out)

    start_carry = (
        jnp.full((q_total, heads_local), NEG_FILL, jnp.float32),
        jnp.zeros((q_total, heads_local), jnp.float32),
        jnp.zeros((q_total, heads_local, head_width), jnp.float32),
    )
    block_order = jnp.arange(local_blocks, dtype=jnp.int32)
    local_peak, local_total, local_out = lax.fori_loop(
        0, local_blocks, partial(visit_block, block_order=block_order), start_carry
    )
    top_peak = lax.pmax(local_peak, "ctx")
    factor = jnp.exp(local_peak - top_peak)
    out_sum, total_sum = lax.psum((local_out * factor[..., None], local_total * factor), "ctx")
    attention = (
        (out_sum / total_sum[..., None])
        .reshape(q_total, heads_local * head_width)
        .astype(jnp.bfloat16)
    )
    return lax.psum_scatter(
        jnp.dot(attention, out_weight, preferred_element_type=jnp.float32),
        "head",
        scatter_dimension=0,
        tiled=True,
    ).astype(jnp.bfloat16)


def solution(mesh):
    return jax.shard_map(
        body,
        mesh=mesh,
        in_specs=(
            P("ctx", "head"),
            P("ctx", "head", None),
            P("ctx", "head", None),
            P("head", None),
            P("head", None),
            P("head", "ctx"),
        ),
        out_specs=P("head", "ctx"),
        check_vma=False,
    )
```

profile of v0, /device:TPU:1, one launch (start us, length us, event | category | flops | bytes accessed | tf_op | source)
XLA Modules:
  0.0 754.8 jit_solution(7034202437298603779)
XLA Ops:
  6.5 0.7 all-gather.2.cloned.1.call-update
  7.4 0.8 compare_reduce_fusion.1
  8.2 1.4 compare_reduce_fusion
  9.7 83.7 %all-gather.2.cloned.1.call-done = bf16[512,1024]{1,0:T(8,128)(2,1)} async-done(((bf16[8,1024]{1,0:T(8,128)(2,1)}), bf16[512,1024]{1,0:T(8,128)(2,1)}) %all-gather.2.cloned.1.call-update) | async-done | bytes 1048592 | tf_op jit(solution)/shard_map/all_gather | solution.py:43
  93.5 2.3 copy.18
  95.8 1.6 copy.20
  97.4 60.9 %while.20 = (s32[]{:T(128)}, f32[512,8]{0,1:T(8,128)S(1)}, f32[512,8]{0,1:T(8,128)S(1)}, f32[512,8,128]{0,2,1:T(8,128)S(1)}, s32[8]{0:T(128)S(1)}, /*index=5*/pr...) while((s32[]{:T(128)}, f32[512,8]{0,1:T(8,128)S(1)}, ...), condition=%wide.region_5.6_spmd.clone, body=%wide.region_2.5_spmd.clone.sunk | while | flops 279020160 | bytes 12146040 | solution.py:89
  97.4 0.7 dynamic_slice.59
  101.1 1.3 fusion.38
  103.1 1.9 fusion.40
  105.0 0.7 dynamic_slice.59
  108.7 1.3 fusion.38
  110.7 1.9 fusion.40
  116.3 1.3 fusion.38
  118.3 1.9 fusion.40
  123.9 1.3 fusion.38
  125.9 1.9 fusion.40
  131.5 1.3 fusion.38
  133.5 1.9 fusion.40
  139.1 1.3 fusion.38
  141.1 1.9 fusion.40
  146.7 1.3 fusion.38
  148.7 1.9 fusion.40
  154.4 1.3 fusion.38
  156.3 1.9 fusion.40
  158.3 221.7 %pmax.7 = f32[512,8]{0,1:T(8,128)S(1)} all-reduce(f32[512,8]{0,1:T(8,128)S(1)} %get-tuple-element.262), channel_id=1, replica_groups=mesh['ctx'=64,'head'=8] {'ctx'}, use_global_device_ids=true, to_apply=%region_6.7 | all-reduce | flops 4096 | bytes 32768 | tf_op jit(solution)/shard_map/pmax | solution.py:92
  380.0 1.6 broadcast_multiply_fusion
  381.7 219.7 %psum.15 = f32[512,8]{0,1:T(8,128)S(1)} all-reduce(f32[512,8]{0,1:T(8,128)S(1)} %get-tuple-element.363), channel_id=1, replica_groups=mesh['ctx'=64,'head'=8] {'ctx'}, use_global_device_ids=true, to_apply=%region_8.9 | all-reduce | flops 4096 | bytes 32768 | tf_op jit(solution)/shard_map/psum | solution.py:94
  601.5 1.9 divide_convert_fusion
  603.3 1.2 fusion.28
  604.5 142.4 %reduce-scatter.2.cloned.1.call-done = f32[64,128]{1,0:T(8,128)} async-done(((f32[512,128]{1,0:T(8,128)}), f32[64,128]{1,0:T(8,128)}) %reduce-scatter.2.cloned.1.call-update) | async-done | bytes 32784 | tf_op jit(solution)/shard_map/reduce_scatter | solution.py:100
  746.9 1.4 convert_element_type.36
  (88 shorter events, 10.8 us)
Async XLA Ops:
  6.5 596.8 %copy-start = (bf16[1024,128]{1,0:T(8,128)(2,1)S(1)}, bf16[1024,128]{1,0:T(8,128)(2,1)}, u32[]{:S(2)}) copy-start(bf16[1024,128]{1,0:T(8,128)(2,1)} %param.13) | copy-start | bytes 786436
  6.5 86.9 %all-gather.2.cloned.1.call-start = ((), (), s32[]{:S(2)}) async-start(), calls=%async_computation.1 | async-start | bytes 1064960 | tf_op jit(solution)/shard_map/all_gather | solution.py:43
  7.3 594.2 %all-reduce.2.cloned.1.call-start = ((), (), s32[]{:S(2)}) async-start(), calls=%async_computation.2 | async-start | bytes 4194304 | tf_op jit(solution)/shard_map/psum | solution.py:94
  381.7 365.2 %reduce-scatter.2.cloned.1.call-start = ((), (), s32[]{:S(2)}) async-start(), calls=%async_computation.3 | async-start | bytes 294912 | tf_op jit(solution)/shard_map/reduce_scatter | solution.py:100
Sparse Core Ops, SparseCore 0:
  10.4 82.9 all-gather.1
  381.8 213.2 all-reduce.1
  604.7 142.2 reduce-scatter.1
where the time goes:
time: 757 us; the launch traced here: 755 us
  blocking collectives  441 us (58%)
  waiting for transfers between devices  227 us (30%)
  matrix products  27.4 us (4%)
  loops' own time  22.9 us (3%)
  between operations  13.2 us (2%)
  other arithmetic  12.9 us (2%)
  local copies, waits for them, and re-layouts  10 us (1%)
    pmax x1, blocking collectives, body(): top_peak = lax.pmax(local_peak, 'ctx')  222 us
    psum x1, blocking collectives, body(): lax.psum((local_out * factor[..., None], local_total * factor), 'ctx')  220 us
    reduce_scatter x1, waiting for transfers between devices, body(): lax.psum_scatter(jnp.dot(attention, out_weight, preferred_element_type=jn...  142 us
    all_gather x1, waiting for transfers between devices, body(): q_whole = lax.all_gather(queries, 'ctx', axis=0, tiled=True)  83.7 us
    another operation x1, loops' own time, body(): lax.fori_loop(0, local_blocks, partial(visit_block, block_order=block_ord...  22.9 us
    dot_general x8, matrix products, block_terms(): jnp.einsum('qgjk,kgd->qgjd', weights_four, value_block, preferred_element...  15.5 us
  transfers between devices with their start and end apart: 3, of which 2 were waited for; matrix products, arithmetic and copies ran while one was open for 0% of the time, Pallas kernels for 0%

commit v1 on v0

v1 whole, which is shorter than its diff:
```python
import functools
import math

import jax
import jax.numpy as jnp
from jax import lax
from jax.experimental import pallas as pl
from jax.experimental.pallas import tpu as pltpu
from jax.sharding import PartitionSpec as P

MESH = pl.DeviceIdType.MESH
BF16, F32 = jnp.bfloat16, jnp.float32
NEG = -1e30
R = 8
ORDER = (4, 3, 5, 2, 6, 1, 7)
GROUPS = 2
NH = 4 // GROUPS
KINDS = (0, 1)
ROWS1 = NH * 64 + 16
PIECE = NH * 8
PARTS = 64 // PIECE
ROWS2 = PIECE + 16


def dot(a, b):
    return jnp.dot(a, b, preferred_element_type=F32)


def pack_stats(top, low, rest):
    return jnp.concatenate([jnp.where(lax.broadcasted_iota(jnp.int32, (8, 128), 1) < 64, top, low), rest], 0)


def split3(x):
    hi = x.astype(BF16).astype(F32)
    mid = (x - hi).astype(BF16).astype(F32)
    return hi, mid, (x - hi) - mid


def unpack_stats(block):
    block = block.astype(F32)
    first = block[:8]
    other = pltpu.roll(first, 64, 1)
    lane = lax.broadcasted_iota(jnp.int32, (8, 128), 1)
    hi = jnp.where(lane < 64, first, other)
    mid = jnp.where(lane < 64, other, first)
    return hi + (mid + block[8:])


def kernel(
    q_ref, k_hbm, v_hbm, vert_ref, slash_ref, w_hbm, o_ref,
    k_in, v_ext, w_ref, kt, bias, tri, qbuf, stat,
    snd1, rcv1, snd2, rcv2, wcol, attn, proj, snd3, rcv3,
    load_sem, send_sem, recv_sem,
):
    ctx, hd = lax.axis_index("ctx"), lax.axis_index("head")
    z, y = ctx // R, ctx % R
    heads = q_ref.shape[1] // 128

    def along(axis, k):
        return {"ctx": z * R + (y + k) % R} if axis == 0 else {"ctx": (z + k) % R * R + y}

    def place(axis):
        return y if axis == 0 else z

    barrier = pltpu.get_barrier_semaphore()
    for k in ORDER:
        for axis in (0, 1):
            pl.semaphore_signal(barrier, inc=1, device_id=along(axis, k), device_id_type=MESH)
        pl.semaphore_signal(barrier, inc=1, device_id={"head": (hd + k) % R}, device_id_type=MESH)

    loads = [
        pltpu.make_async_copy(k_hbm, k_in, load_sem.at[0]),
        pltpu.make_async_copy(v_hbm, v_ext.at[:, pl.ds(0, 128)], load_sem.at[1]),
        pltpu.make_async_copy(w_hbm, w_ref, load_sem.at[2]),
    ]
    for copy in loads:
        copy.start()
    for h in range(heads):
        qbuf[h, z, y] = q_ref[:, h * 128 : (h + 1) * 128]

    pl.semaphore_wait(barrier, 3 * (R - 1))

    def send(src, dst, slot, device):
        copy = pltpu.make_async_remote_copy(
            src_ref=src, dst_ref=dst, send_sem=send_sem.at[slot], recv_sem=recv_sem.at[slot],
            device_id=device, device_id_type=MESH,
        )
        copy.start()

    pending = []

    def arrived(like, slot):
        copy = pltpu.make_async_remote_copy(
            src_ref=like, dst_ref=like, send_sem=send_sem.at[slot], recv_sem=recv_sem.at[slot],
            device_id=along(0, 1), device_id_type=MESH,
        )
        copy.wait_recv()
        pending.append(copy)

    def slot(phase, kind, group):
        return (phase * 2 + kind) * GROUPS + group

    def head_span(kind, group):
        return pl.ds(kind * 4 + group * NH, NH)

    def q1_send(group):
        for k in ORDER:
            for kind in KINDS:
                ref = qbuf.at[head_span(kind, group), z, y]
                send(ref, ref, slot(0, kind, group), along(kind, k))

    def q1_wait(group):
        for kind in KINDS:
            arrived(qbuf.at[head_span(kind, group), 0, pl.ds(0, R - 1)], slot(0, kind, group))

    def q2_send(group):
        for k in ORDER:
            for kind in KINDS:
                span = head_span(kind, group)
                ref = qbuf.at[span, z] if kind == 0 else qbuf.at[span, :, y]
                send(ref, ref, slot(1, kind, group), along(1 - kind, k))

    def q2_wait(group):
        for kind in KINDS:
            arrived(qbuf.at[head_span(kind, group), pl.ds(0, R - 1)], slot(1, kind, group))

    lane = lax.broadcasted_iota(jnp.int32, (8, 128), 1)
    sub = lax.broadcasted_iota(jnp.int32, (8, 128), 0)
    scale = math.log2(math.e) / math.sqrt(128.0)

    def prepare():
        first = 508 - 8 * ctx
        vert, slash = vert_ref[...], slash_ref[...]
        by_slash = {
            d: jnp.max(jnp.where(slash == first + d, 1.0, 0.0), axis=1, keepdims=True) for d in range(-7, 4)
        }
        by_vert = [jnp.max(jnp.where(vert == 8 * ctx + j, 1.0, 0.0), axis=1, keepdims=True) for j in range(8)]
        for b in range(4):
            for j in range(8):
                hit = jnp.maximum(by_slash[b - j], by_vert[j])
                row = jnp.broadcast_to(jnp.where(hit > 0.5, 0.0, NEG), (heads, 128))
                if j > b + 4:
                    row = jnp.where(ctx == R * R - 1, NEG, row)
                bias[:, b, j * 128 : (j + 1) * 128] = row
        r128 = lax.broadcasted_iota(jnp.int32, (128, 128), 0)
        c128 = lax.broadcasted_iota(jnp.int32, (128, 128), 1)
        tri[...] = jnp.where((c128 <= r128) | (ctx != R * R - 1), 0.0, NEG)
        v_ext[:, 128:] = jnp.ones((v_ext.shape[0], 128), BF16)
        stat[...] = jnp.zeros_like(stat)
        for copy in loads:
            copy.wait()
        kt[...] = k_in[...].astype(F32).T.astype(BF16)

    def attend(kind, group):
        def one_head(hh, _):
            h = kind * 4 + group * NH + hh
            limits = bias[h]
            for b in range(4):
                q = qbuf[h, 2 * b : 2 * b + 2].reshape(128, 128)
                s = dot(q, kt[...]) * scale + limits[b : b + 1, :]
                c = (4 + b) * 128
                diag = s[:, c : c + 128] + tri[...]
                parts = [s[:, :c], diag] + ([s[:, c + 128 :]] if b < 3 else [])
                s = jnp.concatenate(parts, axis=1)
                m = jnp.max(s, axis=1, keepdims=True)
                p = jnp.exp2(s - m).astype(BF16)
                out = dot(p, v_ext[...])
                total = out[:, 128:]
                mean = (out[:, :128] / total).astype(BF16)
                snd1[kind, group, 2 * b : 2 * b + 2, pl.ds(pl.multiple_of(hh * 64, 64), 64), :] = mean.reshape(2, 64, 128)
                lse = m + jnp.log2(total)
                rows = slice(b * 128, (b + 1) * 128)
                at = lax.broadcasted_iota(jnp.int32, (128, 128), 1)
                stat[rows, :] = jnp.where(at == hh, lse, stat[rows, :])
            return 0

        lax.fori_loop(0, NH, one_head, 0)
        for b in range(4):
            block = stat[b * 128 : (b + 1) * 128, :].T[:8]
            hi, mid, lo = split3(block)
            turned = [pltpu.roll(x, 64, 1) for x in (hi, mid, lo)]
            even = pack_stats(hi, turned[1], jnp.where(lane < 64, lo, turned[2]))
            odd = pack_stats(turned[0], mid, jnp.where(lane < 64, turned[2], lo))
            snd1[kind, group, 2 * b, NH * 64 :, :] = even.astype(BF16)
            snd1[kind, group, 2 * b + 1, NH * 64 :, :] = odd.astype(BF16)

    def r1_send(kind, group):
        for k in ORDER:
            to = (place(kind) + k) % R
            send(snd1.at[kind, group, to], rcv1.at[kind, group, k - 1], slot(2, kind, group), along(kind, k))

    def r1_combine(kind, group):
        arrived(rcv1.at[kind, group], slot(2, kind, group))
        own = snd1.at[kind, group, place(kind)]
        refs = [own] + [rcv1.at[kind, group, k] for k in range(R - 1)]
        logs = [unpack_stats(ref[NH * 64 :, :]) for ref in refs]
        top = functools.reduce(jnp.maximum, logs)
        raised = [jnp.exp2(x - top) for x in logs]
        total = functools.reduce(jnp.add, raised)
        cols = jnp.concatenate([x / total for x in raised] + [jnp.zeros((64, 128), F32)], 0).T
        for hh in range(NH):
            acc = None
            for s, ref in enumerate(refs):
                term = cols[:64, s * 8 + hh : s * 8 + hh + 1] * ref[hh * 64 : (hh + 1) * 64, :].astype(F32)
                acc = term if acc is None else acc + term
            acc = acc.astype(BF16).reshape(PARTS, PIECE, 128)
            snd2[kind, group, hh * PARTS : (hh + 1) * PARTS, :PIECE, :] = acc
        hi, mid, lo = split3(top + jnp.log2(total))
        packed = pack_stats(hi, mid, lo).astype(BF16)
        for to in range(R):
            snd2[kind, group, to, PIECE:, :] = packed

    def r2_send(kind, group):
        axis = 1 - kind
        for k in ORDER:
            to = (place(axis) + k) % R
            send(snd2.at[kind, group, to], rcv2.at[kind, group, k - 1], slot(3, kind, group), along(axis, k))

    def own_piece(kind, group):
        axis = 1 - kind
        me = place(axis)
        start = pl.multiple_of(me % PARTS * PIECE, PIECE)
        return attn.at[kind, group, place(kind), me // PARTS, pl.ds(start, PIECE)]

    def r2_combine(kind, group):
        arrived(rcv2.at[kind, group], slot(3, kind, group))
        me = place(1 - kind)
        hh, part = me // PARTS, me % PARTS
        refs = [snd2.at[kind, group, me]] + [rcv2.at[kind, group, k] for k in range(R - 1)]
        logs = jnp.zeros((8, 128), F32)
        for s, ref in enumerate(refs):
            row = jnp.sum(jnp.where(sub == hh, unpack_stats(ref[PIECE:, :]), 0.0), axis=0, keepdims=True)
            logs = jnp.where(sub == s, row, logs)
        raised = jnp.exp2(logs - jnp.max(logs, axis=0, keepdims=True))
        weight = raised / jnp.sum(raised, axis=0, keepdims=True)
        wcol[...] = jnp.concatenate([weight, jnp.zeros((120, 128), F32)], 0).T
        cols = wcol[pl.ds(pl.multiple_of(part * PIECE, PIECE), PIECE), :]
        acc = None
        for s, ref in enumerate(refs):
            term = cols[:, s : s + 1] * ref[:PIECE, :].astype(F32)
            acc = term if acc is None else acc + term
        own_piece(kind, group)[...] = acc.astype(BF16)

    def g1_send(kind, group):
        for k in ORDER:
            ref = own_piece(kind, group)
            send(ref, ref, slot(4, kind, group), along(1 - kind, k))

    def g1_wait(kind, group):
        arrived(rcv2.at[kind, group, :, pl.ds(0, PIECE)], slot(4, kind, group))

    def g2_send(kind, group):
        ref = attn.at[kind, group, place(kind)]
        for k in ORDER:
            send(ref, ref, slot(5, kind, group), along(kind, k))

    def g2_wait(kind, group):
        arrived(attn.at[kind, group, pl.ds(0, R - 1)], slot(5, kind, group))

    def project(kind, group):
        acc = None
        for hh in range(0, NH, 2):
            left = [attn[kind, group, :, hh + i].reshape(512, 128) for i in range(2)]
            row = (kind * 4 + group * NH + hh) * 128
            term = dot(jnp.concatenate(left, 1), w_ref[row : row + 256, :])
            acc = term if acc is None else acc + term
        return acc

    every = [(kind, group) for group in range(GROUPS) for kind in KINDS]
    for group in range(GROUPS):
        q1_send(group)
    prepare()
    for group in range(GROUPS):
        q1_wait(group)
        q2_send(group)
    for group in range(GROUPS):
        q2_wait(group)
        for kind in KINDS:
            attend(kind, group)
            r1_send(kind, group)
    for group in range(GROUPS):
        for kind in KINDS:
            r1_combine(kind, group)
            r2_send(kind, group)
        for kind in KINDS:
            r2_combine(kind, group)
            g1_send(kind, group)
        if group:
            for kind in KINDS:
                g1_wait(kind, group - 1)
                g2_send(kind, group - 1)
    for kind in KINDS:
        g1_wait(kind, GROUPS - 1)
        g2_send(kind, GROUPS - 1)
    total = None
    for kind, group in every:
        g2_wait(kind, group)
        term = project(kind, group)
        total = term if total is None else total + term
    proj[...] = total
    snd3[...] = total.astype(BF16).reshape(R, 64, 128)
    last = slot(6, 0, 0)
    for k in ORDER:
        to = (hd + k) % R
        send(snd3.at[to], rcv3.at[k - 1], last, {"head": to})
    arrived(rcv3, last)
    out = proj[pl.ds(pl.multiple_of(hd * 64, 64), 64), :]
    for k in range(R - 1):
        out = out + rcv3[k].astype(F32)
    o_ref[...] = out.astype(BF16)
    for copy in pending:
        copy.wait_send()


def body(queries, cache_keys, cache_values, vertical_blocks, slash_offsets, out_weight):
    keys, values = cache_keys[:, 0, :], cache_values[:, 0, :]
    local, width = keys.shape
    heads = vertical_blocks.shape[0]
    slots = 6 * 2 * GROUPS + 1
    vmem, hbm = pl.BlockSpec(memory_space=pltpu.VMEM), pl.BlockSpec(memory_space=pl.ANY)
    return pl.pallas_call(
        kernel,
        out_shape=jax.ShapeDtypeStruct((64, 128), BF16),
        in_specs=[vmem, hbm, hbm, vmem, vmem, hbm],
        out_specs=vmem,
        scratch_shapes=[
            pltpu.VMEM((local, width), BF16),
            pltpu.VMEM((local, 256), BF16),
            pltpu.VMEM(out_weight.shape, BF16),
            pltpu.VMEM((width, local), BF16),
            pltpu.VMEM((heads, 4, local), F32),
            pltpu.VMEM((128, 128), F32),
            pltpu.VMEM((heads, R, R, 8, 128), BF16),
            pltpu.VMEM((512, 128), F32),
            pltpu.VMEM((2, GROUPS, R, ROWS1, 128), BF16),
            pltpu.VMEM((2, GROUPS, R - 1, ROWS1, 128), BF16),
            pltpu.VMEM((2, GROUPS, R, ROWS2, 128), BF16),
            pltpu.VMEM((2, GROUPS, R - 1, ROWS2, 128), BF16),
            pltpu.VMEM((128, 128), F32),
            pltpu.VMEM((2, GROUPS, R, NH, 64, 128), BF16),
            pltpu.VMEM((512, 128), F32),
            pltpu.VMEM((R, 64, 128), BF16),
            pltpu.VMEM((R - 1, 64, 128), BF16),
            pltpu.SemaphoreType.DMA((3,)),
            pltpu.SemaphoreType.DMA((slots,)),
            pltpu.SemaphoreType.DMA((slots,)),
        ],
        compiler_params=pltpu.CompilerParams(
            collective_id=0, has_side_effects=True, vmem_limit_bytes=48 * 1024 * 1024
        ),
    )(queries, keys, values, vertical_blocks, slash_offsets, out_weight)


def solution(mesh):
    return jax.shard_map(
        body,
        mesh=mesh,
        in_specs=(
            P("ctx", "head"),
            P("ctx", "head", None),
            P("ctx", "head", None),
            P("head", None),
            P("head", None),
            P("head", "ctx"),
        ),
        out_specs=P("head", "ctx"),
        check_vma=False,
    )
```

time: 757 us -> 78.6 us (0.10)
  blocking collectives: 441 us -> 0 us
  waiting for transfers between devices: 227 us -> 0 us
  Pallas kernels: 0 us -> 72.7 us
  matrix products: 27.4 us -> 0 us
  loops' own time: 22.9 us -> 0 us
  between operations: 13.2 us -> 0.02 us
  other arithmetic: 12.9 us -> 0 us
    pmax x1 -> x0, blocking collectives: 222 us -> none  [body(): top_peak = lax.pmax(local_peak, 'ctx')]
    psum x1 -> x0, blocking collectives: 220 us -> none  [body(): lax.psum((local_out * factor[..., None], local_total * factor), 'ctx')]
    reduce_scatter x1 -> x0, waiting for transfers between devices: 142 us -> none  [body(): lax.psum_scatter(jnp.dot(attention, out_weight, preferred_element_type=jn...]
    all_gather x1 -> x0, waiting for transfers between devices: 83.7 us -> none  [body(): q_whole = lax.all_gather(queries, 'ctx', axis=0, tiled=True)]
    pallas_call x0 -> x1, Pallas kernels: none -> 72.7 us  [body(): pl.pallas_call(kernel, out_shape=jax.ShapeDtypeStruct((64, 128), BF16), i...]
    dot_general x17 -> x0, matrix products: 27.4 us -> none  [the longest x8 15.5 us: block_terms(): jnp.einsum('qgjk,kgd->qgjd', weights_four, value_block, preferred_element...]
    another operation x1 -> x0, loops' own time: 22.9 us -> none  [body(): lax.fori_loop(0, local_blocks, partial(visit_block, block_order=block_ord...]
  transfers between devices with their start and end apart: 3 -> 0, of which waited for: 2 -> 0; matrix products, arithmetic and copies ran while one was open for 0% -> 0% of each run, Pallas kernels for 0% -> 0%
where the time goes in v1:
time: 78.6 us; the launch traced here: 78.3 us
  Pallas kernels  72.7 us (92%)
  local copies, waits for them, and re-layouts  5.55 us (7%)
    pallas_call x1, Pallas kernels, body(): pl.pallas_call(kernel, out_shape=jax.ShapeDtypeStruct((64, 128), BF16), i...  72.7 us
    unnamed x13, local copies, waits for them, and re-layouts  5.55 us

profile of v1, /device:TPU:1, one launch (start us, length us, event | category | flops | bytes accessed | tf_op | source)
XLA Modules:
  0.0 78.3 jit_solution(2078874164543689357)
XLA Ops:
  0.0 0.0 copy-start
  0.0 0.9 %copy-done = bf16[1024,1,128]{2,0,1:T(8,128)(2,1)S(1)} copy-done((bf16[1024,1,128]{2,0,1:T(8,128)(2,1)S(1)}, bf16[1024,1,128]{2,0,1:T(8,128)(2,1)}, u32[]{:S(2)}) %copy-start) | copy-done | bytes 262168
  1.0 0.0 copy-start.1
  1.0 0.9 %copy-done.1 = bf16[1024,1,128]{2,0,1:T(8,128)(2,1)S(1)} copy-done((bf16[1024,1,128]{2,0,1:T(8,128)(2,1)S(1)}, bf16[1024,1,128]{2,0,1:T(8,128)(2,1)}, u32[]{:S(2)}) %copy-start.1) | copy-done | bytes 262168
  1.9 0.0 copy-start.2
  1.9 0.9 %copy-done.2 = bf16[1024,128]{1,0:T(8,128)(2,1)S(1)} copy-done((bf16[1024,128]{1,0:T(8,128)(2,1)S(1)}, bf16[1024,128]{1,0:T(8,128)(2,1)}, u32[]{:S(2)}) %copy-start.2) | copy-done | bytes 262168
  2.9 0.0 copy-start.3
  2.9 0.7 copy-done.3
  3.6 0.0 copy-start.4
  3.6 0.7 copy-done.4
  4.3 0.0 copy-start.5
  4.3 0.7 copy-done.5
  4.9 72.7 %shard_map.64 = bf16[64,128]{1,0:T(8,128)(2,1)S(1)} custom-call(bf16[8,1024]{1,0:T(8,128)(2,1)S(1)} %copy-done.3, bf16[1024,128]{1,0:T(8,128)(2,1)S(1)} %bitcast.2, bf16[1024,128]{1,0:T(8,128)(2,1)S(1)} %bitcast.3, s32[8,8]{1,0:T(8,128)S(1)} %copy-done.4, s32[8,48]{1,0:T(8,128)S(1)} %copy-done.5, bf16[1024,128]{1,0:T(8,128)(2,1)S(1)} %copy-done.2), custom_call_target="tpu_custom_call" | custom-call | tf_op jit(solution)/shard_map/pallas_call | solution.py:321
  77.7 0.6 copy.8
Async XLA Ops:
  0.0 0.9 %copy-start = (bf16[1024,1,128]{2,0,1:T(8,128)(2,1)S(1)}, bf16[1024,1,128]{2,0,1:T(8,128)(2,1)}, u32[]{:S(2)}) copy-start(bf16[1024,1,128]{2,0,1:T(8,128)(2,1)} %param.7) | copy-start | bytes 786436
  1.0 0.9 %copy-start.1 = (bf16[1024,1,128]{2,0,1:T(8,128)(2,1)S(1)}, bf16[1024,1,128]{2,0,1:T(8,128)(2,1)}, u32[]{:S(2)}) copy-start(bf16[1024,1,128]{2,0,1:T(8,128)(2,1)} %param.8) | copy-start | bytes 786436
  1.9 0.9 %copy-start.2 = (bf16[1024,128]{1,0:T(8,128)(2,1)S(1)}, bf16[1024,128]{1,0:T(8,128)(2,1)}, u32[]{:S(2)}) copy-start(bf16[1024,128]{1,0:T(8,128)(2,1)} %w_hbm.1) | copy-start | bytes 786436
  2.9 0.7 copy-start.3
  3.6 0.7 copy-start.4
  4.3 0.7 copy-start.5

commit v2 on v1

--- a/solution.py
+++ b/solution.py
@@ -47,14 +47,14 @@
 
 
 def kernel(
-    q_ref, k_hbm, v_hbm, vert_ref, slash_ref, w_hbm, o_ref,
-    k_in, v_ext, w_ref, kt, bias, tri, qbuf, stat,
+    q_hbm, k_hbm, v_hbm, vert_hbm, slash_hbm, w_hbm, o_ref,
+    q_in, vert_in, slash_in, k_in, v_ext, w_ref, ktx, tri, qbuf, score, prob, stat,
     snd1, rcv1, snd2, rcv2, wcol, attn, proj, snd3, rcv3,
     load_sem, send_sem, recv_sem,
 ):
     ctx, hd = lax.axis_index("ctx"), lax.axis_index("head")
     z, y = ctx // R, ctx % R
-    heads = q_ref.shape[1] // 128
+    heads = q_in.shape[1] // 128
 
     def along(axis, k):
         return {"ctx": z * R + (y + k) % R} if axis == 0 else {"ctx": (z + k) % R * R + y}
@@ -62,21 +62,30 @@
     def place(axis):
         return y if axis == 0 else z
 
+    loads = [
+        pltpu.make_async_copy(src, dst, load_sem.at[i])
+        for i, (src, dst) in enumerate(
+            [
+                (q_hbm, q_in),
+                (vert_hbm, vert_in),
+                (slash_hbm, slash_in),
+                (k_hbm, k_in),
+                (v_hbm, v_ext.at[:, pl.ds(0, 128)]),
+                (w_hbm, w_ref),
+            ]
+        )
+    ]
+    for copy in loads:
+        copy.start()
     barrier = pltpu.get_barrier_semaphore()
     for k in ORDER:
         for axis in (0, 1):
             pl.semaphore_signal(barrier, inc=1, device_id=along(axis, k), device_id_type=MESH)
         pl.semaphore_signal(barrier, inc=1, device_id={"head": (hd + k) % R}, device_id_type=MESH)
 
-    loads = [
-        pltpu.make_async_copy(k_hbm, k_in, load_sem.at[0]),
-        pltpu.make_async_copy(v_hbm, v_ext.at[:, pl.ds(0, 128)], load_sem.at[1]),
-        pltpu.make_async_copy(w_hbm, w_ref, load_sem.at[2]),
-    ]
-    for copy in loads:
-        copy.start()
+    loads[0].wait()
     for h in range(heads):
-        qbuf[h, z, y] = q_ref[:, h * 128 : (h + 1) * 128]
+        qbuf[h, z, y] = q_in[:, h * 128 : (h + 1) * 128]
 
     pl.semaphore_wait(barrier, 3 * (R - 1))
 
@@ -98,85 +107,108 @@
         pending.append(copy)
 
     def slot(phase, kind, group):
-        return (phase * 2 + kind) * GROUPS + group
-
-    def head_span(kind, group):
-        return pl.ds(kind * 4 + group * NH, NH)
-
-    def q1_send(group):
+        return (phase * 2 + kind) * 4 + group
+
+    def q1_send():
         for k in ORDER:
             for kind in KINDS:
-                ref = qbuf.at[head_span(kind, group), z, y]
-                send(ref, ref, slot(0, kind, group), along(kind, k))
-
-    def q1_wait(group):
+                ref = qbuf.at[pl.ds(4 * kind, 4), z, y]
+                send(ref, ref, slot(0, kind, 0), along(kind, k))
+
+    def q1_wait():
         for kind in KINDS:
-            arrived(qbuf.at[head_span(kind, group), 0, pl.ds(0, R - 1)], slot(0, kind, group))
-
-    def q2_send(group):
+            arrived(qbuf.at[pl.ds(4 * kind, 4), 0, pl.ds(0, R - 1)], slot(0, kind, 0))
+
+    def q2_send(pair):
         for k in ORDER:
             for kind in KINDS:
-                span = head_span(kind, group)
-                ref = qbuf.at[span, z] if kind == 0 else qbuf.at[span, :, y]
-                send(ref, ref, slot(1, kind, group), along(1 - kind, k))
-
-    def q2_wait(group):
+                h = 4 * kind + pair
+                ref = qbuf.at[h, z] if kind == 0 else qbuf.at[h, :, y]
+                send(ref, ref, slot(1, kind, pair), along(1 - kind, k))
+
+    def q2_wait(pair):
         for kind in KINDS:
-            arrived(qbuf.at[head_span(kind, group), pl.ds(0, R - 1)], slot(1, kind, group))
+            arrived(qbuf.at[4 * kind + pair, pl.ds(0, R - 1)], slot(1, kind, pair))
 
     lane = lax.broadcasted_iota(jnp.int32, (8, 128), 1)
     sub = lax.broadcasted_iota(jnp.int32, (8, 128), 0)
     scale = math.log2(math.e) / math.sqrt(128.0)
 
     def prepare():
+        for copy in loads[1:]:
+            copy.wait()
+        v_ext[:, 128:] = jnp.ones((v_ext.shape[0], 128), BF16)
+        stat[...] = jnp.zeros_like(stat)
+        kt = k_in[...].astype(F32).T.astype(BF16)
+        for h in range(heads):
+            ktx[h, :128, :] = kt
+
+    def prepare_masks():
         first = 508 - 8 * ctx
-        vert, slash = vert_ref[...], slash_ref[...]
+        vert, slash = vert_in[...], slash_in[...]
         by_slash = {
             d: jnp.max(jnp.where(slash == first + d, 1.0, 0.0), axis=1, keepdims=True) for d in range(-7, 4)
         }
         by_vert = [jnp.max(jnp.where(vert == 8 * ctx + j, 1.0, 0.0), axis=1, keepdims=True) for j in range(8)]
+        masks = []
         for b in range(4):
+            blocks = []
             for j in range(8):
                 hit = jnp.maximum(by_slash[b - j], by_vert[j])
                 row = jnp.broadcast_to(jnp.where(hit > 0.5, 0.0, NEG), (heads, 128))
                 if j > b + 4:
                     row = jnp.where(ctx == R * R - 1, NEG, row)
-                bias[:, b, j * 128 : (j + 1) * 128] = row
+                blocks.append(row)
+            masks.append(jnp.concatenate(blocks, 1))
+        local = masks[0].shape[1]
+        for h in range(heads):
+            rows = [mask[h : h + 1, :] for mask in masks] + [jnp.zeros((124, local), F32)]
+            ktx[h, 128:, :] = jnp.concatenate(rows, 0).astype(BF16)
         r128 = lax.broadcasted_iota(jnp.int32, (128, 128), 0)
         c128 = lax.broadcasted_iota(jnp.int32, (128, 128), 1)
         tri[...] = jnp.where((c128 <= r128) | (ctx != R * R - 1), 0.0, NEG)
-        v_ext[:, 128:] = jnp.ones((v_ext.shape[0], 128), BF16)
-        stat[...] = jnp.zeros_like(stat)
-        for copy in loads:
-            copy.wait()
-        kt[...] = k_in[...].astype(F32).T.astype(BF16)
-
-    def attend(kind, group):
-        def one_head(hh, _):
-            h = kind * 4 + group * NH + hh
-            limits = bias[h]
-            for b in range(4):
-                q = qbuf[h, 2 * b : 2 * b + 2].reshape(128, 128)
-                s = dot(q, kt[...]) * scale + limits[b : b + 1, :]
-                c = (4 + b) * 128
-                diag = s[:, c : c + 128] + tri[...]
-                parts = [s[:, :c], diag] + ([s[:, c + 128 :]] if b < 3 else [])
-                s = jnp.concatenate(parts, axis=1)
-                m = jnp.max(s, axis=1, keepdims=True)
-                p = jnp.exp2(s - m).astype(BF16)
-                out = dot(p, v_ext[...])
-                total = out[:, 128:]
-                mean = (out[:, :128] / total).astype(BF16)
-                snd1[kind, group, 2 * b : 2 * b + 2, pl.ds(pl.multiple_of(hh * 64, 64), 64), :] = mean.reshape(2, 64, 128)
-                lse = m + jnp.log2(total)
-                rows = slice(b * 128, (b + 1) * 128)
-                at = lax.broadcasted_iota(jnp.int32, (128, 128), 1)
-                stat[rows, :] = jnp.where(at == hh, lse, stat[rows, :])
-            return 0
-
-        lax.fori_loop(0, NH, one_head, 0)
+
+    def scores(kind, pair):
+        row = lax.broadcasted_iota(jnp.int32, (512, 128), 0) // 128
+        chooser = jnp.where(lax.broadcasted_iota(jnp.int32, (512, 128), 1) == row, 1.0, 0.0).astype(BF16)
+        h = 4 * kind + pair
+        score[kind] = dot(jnp.concatenate([qbuf[h].reshape(512, 128), chooser], 1), ktx[h])
+
+    def weigh(kind):
+        tops = []
         for b in range(4):
-            block = stat[b * 128 : (b + 1) * 128, :].T[:8]
+            rows = slice(b * 128, (b + 1) * 128)
+            c = (4 + b) * 128
+            s = score[kind, rows]
+            parts = [s[:, :c], s[:, c : c + 128] + tri[...]] + ([s[:, c + 128 :]] if b < 3 else [])
+            s = jnp.concatenate(parts, axis=1)
+            top = jnp.max(s, axis=1, keepdims=True) * scale
+            prob[kind, rows] = jnp.exp2(s * scale - top).astype(BF16)
+            tops.append(top)
+        return tops
+
+    def finish(kind, pair, tops):
+        group, hh = pair // NH, pair % NH
+        for b in range(4):
+            rows = slice(b * 128, (b + 1) * 128)
+            out = dot(prob[kind, rows], v_ext[...])
+            total = out[:, 128:]
+            mean = (out[:, :128] / total).astype(BF16)
+            snd1[kind, group, 2 * b : 2 * b + 2, hh * 64 : (hh + 1) * 64, :] = mean.reshape(2, 64, 128)
+            at = lax.broadcasted_iota(jnp.int32, (128, 128), 1)
+            stat[kind, rows] = jnp.where(at == hh, tops[b] + jnp.log2(total), stat[kind, rows])
+
+    def attend(pair):
+        scores(0, pair)
+        tops0 = weigh(0)
+        scores(1, pair)
+        finish(0, pair, tops0)
+        tops1 = weigh(1)
+        finish(1, pair, tops1)
+
+    def statistics(kind, group):
+        for b in range(4):
+            block = stat[kind, b * 128 : (b + 1) * 128, :].T[:8]
             hi, mid, lo = split3(block)
             turned = [pltpu.roll(x, 64, 1) for x in (hi, mid, lo)]
             even = pack_stats(hi, turned[1], jnp.where(lane < 64, lo, turned[2]))
@@ -266,48 +298,39 @@
             acc = term if acc is None else acc + term
         return acc
 
-    every = [(kind, group) for group in range(GROUPS) for kind in KINDS]
-    for group in range(GROUPS):
-        q1_send(group)
-    prepare()
-    for group in range(GROUPS):
-        q1_wait(group)
-        q2_send(group)
-    for group in range(GROUPS):
-        q2_wait(group)
-        for kind in KINDS:
-            attend(kind, group)
-            r1_send(kind, group)
-    for group in range(GROUPS):
-        for kind in KINDS:
-            r1_combine(kind, group)
-            r2_send(kind, group)
-        for kind in KINDS:
-            r2_combine(kind, group)
-            g1_send(kind, group)
-        if group:
+    def tail():
+        total = None
+        for group in range(GROUPS):
             for kind in KINDS:
-                g1_wait(kind, group - 1)
-                g2_send(kind, group - 1)
-    for kind in KINDS:
-        g1_wait(kind, GROUPS - 1)
-        g2_send(kind, GROUPS - 1)
-    total = None
-    for kind, group in every:
-        g2_wait(kind, group)
-        term = project(kind, group)
-        total = term if total is None else total + term
-    proj[...] = total
-    snd3[...] = total.astype(BF16).reshape(R, 64, 128)
-    last = slot(6, 0, 0)
-    for k in ORDER:
-        to = (hd + k) % R
-        send(snd3.at[to], rcv3.at[k - 1], last, {"head": to})
-    arrived(rcv3, last)
-    out = proj[pl.ds(pl.multiple_of(hd * 64, 64), 64), :]
-    for k in range(R - 1):
-        out = out + rcv3[k].astype(F32)
-    o_ref[...] = out.astype(BF16)
+                g2_wait(kind, group)
+                term = project(kind, group)
+                total = term if total is None else total + term
+        proj[...] = total
+        snd3[...] = total.astype(BF16).reshape(R, 64, 128)
+        last = slot(6, 0, 0)
+        for k in ORDER:
+            to = (hd + k) % R
+            send(snd3.at[to], rcv3.at[k - 1], last, {"head": to})
+        arrived(rcv3, last)
+        out = proj[pl.ds(pl.multiple_of(hd * 64, 64), 64), :]
+        for k in range(R - 1):
+            out = out + rcv3[k].astype(F32)
+        o_ref[...] = out.astype(BF16)
+
+    steps = [(q1_send,), (prepare,), (q1_wait,)]
+    steps += [(q2_send, pair) for pair in range(4)] + [(prepare_masks,)]
+    for pair in range(4):
+        steps += [(q2_wait, pair), (attend, pair)]
+        if pair % NH == NH - 1:
+            for kind in KINDS:
+                steps += [(statistics, kind, pair // NH), (r1_send, kind, pair // NH)]
+    both = [(kind, group) for group in range(GROUPS) for kind in KINDS]
+    for first, second in ((r1_combine, r2_send), (r2_combine, g1_send), (g1_wait, g2_send)):
+        for args in both:
+            steps += [(first, *args), (second, *args)]
+    steps += [(tail,)]
+    for step, *args in steps:
+        step(*args)
     for copy in pending:
         copy.wait_send()
 
@@ -316,22 +339,26 @@
     keys, values = cache_keys[:, 0, :], cache_values[:, 0, :]
     local, width = keys.shape
     heads = vertical_blocks.shape[0]
-    slots = 6 * 2 * GROUPS + 1
-    vmem, hbm = pl.BlockSpec(memory_space=pltpu.VMEM), pl.BlockSpec(memory_space=pl.ANY)
+    slots = 6 * 2 * 4 + 1
+    vmem, hbm = pl.BlockSpec(memory_space=pltpu.VMEM), pl.BlockSpec(memory_space=pltpu.HBM)
     return pl.pallas_call(
         kernel,
         out_shape=jax.ShapeDtypeStruct((64, 128), BF16),
-        in_specs=[vmem, hbm, hbm, vmem, vmem, hbm],
+        in_specs=[hbm] * 6,
         out_specs=vmem,
         scratch_shapes=[
+            pltpu.VMEM(queries.shape, BF16),
+            pltpu.VMEM(vertical_blocks.shape, jnp.int32),
+            pltpu.VMEM(slash_offsets.shape, jnp.int32),
             pltpu.VMEM((local, width), BF16),
             pltpu.VMEM((local, 256), BF16),
             pltpu.VMEM(out_weight.shape, BF16),
-            pltpu.VMEM((width, local), BF16),
-            pltpu.VMEM((heads, 4, local), F32),
+            pltpu.VMEM((heads, 2 * width, local), BF16),
             pltpu.VMEM((128, 128), F32),
             pltpu.VMEM((heads, R, R, 8, 128), BF16),
-            pltpu.VMEM((512, 128), F32),
+            pltpu.VMEM((2, 512, local), F32),
+            pltpu.VMEM((2, 512, local), BF16),
+            pltpu.VMEM((2, 512, 128), F32),
             pltpu.VMEM((2, GROUPS, R, ROWS1, 128), BF16),
             pltpu.VMEM((2, GROUPS, R - 1, ROWS1, 128), BF16),
             pltpu.VMEM((2, GROUPS, R, ROWS2, 128), BF16),
@@ -341,12 +368,12 @@
             pltpu.VMEM((512, 128), F32),
             pltpu.VMEM((R, 64, 128), BF16),
             pltpu.VMEM((R - 1, 64, 128), BF16),
-            pltpu.SemaphoreType.DMA((3,)),
+            pltpu.SemaphoreType.DMA((6,)),
             pltpu.SemaphoreType.DMA((slots,)),
             pltpu.SemaphoreType.DMA((slots,)),
         ],
         compiler_params=pltpu.CompilerParams(
-            collective_id=0, has_side_effects=True, vmem_limit_bytes=48 * 1024 * 1024
+            collective_id=0, has_side_effects=True, vmem_limit_bytes=61 * 1024 * 1024
         ),
     )(queries, keys, values, vertical_blocks, slash_offsets, out_weight)
 

time: 78.6 us -> 72.1 us (0.917)
  local copies, waits for them, and re-layouts: 5.55 us -> 1.32 us
  Pallas kernels: 72.7 us -> 70.5 us
    unnamed x13 -> x1, local copies, waits for them, and re-layouts: 5.55 us -> 1.32 us
    pallas_call x1, Pallas kernels: 72.7 us -> 70.5 us  [body(): pl.pallas_call(kernel, out_shape=jax.ShapeDtypeStruct((64, 128), BF16), i...]
where the time goes in v2:
time: 72.1 us; the launch traced here: 71.8 us
  Pallas kernels  70.5 us (98%)
  local copies, waits for them, and re-layouts  1.32 us (2%)
    pallas_call x1, Pallas kernels, body(): pl.pallas_call(kernel, out_shape=jax.ShapeDtypeStruct((64, 128), BF16), i...  70.5 us

profile of v2, /device:TPU:1, one launch (start us, length us, event | category | flops | bytes accessed | tf_op | source)
XLA Modules:
  0.0 71.8 jit_solution(9229108391010686454)
XLA Ops:
  0.0 70.5 %shard_map.64 = bf16[64,128]{1,0:T(8,128)(2,1)} custom-call(bf16[8,1024]{1,0:T(8,128)(2,1)} %q_hbm.1, bf16[1024,128]{1,0:T(8,128)(2,1)} %bitcast.2, bf16[1024,128]{1,0:T(8,128)(2,1)} %bitcast.3, s32[8,8]{1,0:T(8,128)} %vert_hbm.1, s32[8,48]{1,0:T(8,128)} %slash_hbm.1, bf16[1024,128]{1,0:T(8,128)(2,1)} %w_hbm.1), custom_call_target="tpu_custom_call" | custom-call | tf_op jit(solution)/shard_map/pallas_call | solution.py:344
  70.5 1.3 %copy.8 = bf16[64,128]{1,0:T(8,128)(2,1)} copy(bf16[64,128]{1,0:T(8,128)(2,1)} %shard_map.64) | data formatting | bytes 32768

commit v3 on v2

--- a/solution.py
+++ b/solution.py
@@ -119,16 +119,33 @@
         for kind in KINDS:
             arrived(qbuf.at[pl.ds(4 * kind, 4), 0, pl.ds(0, R - 1)], slot(0, kind, 0))
 
+    def spread(axis, sign, block, direct, final):
+        ref = block(place(axis))
+        for k, where in ((-3 * sign, direct), (2 * sign, direct), (1, final), (-1, final)):
+            send(ref, ref, where, along(axis, k % R))
+
+    def relay(axis, sign, block, direct, final, like):
+        arrived(like, direct)
+        three, two = block((place(axis) + 3 * sign + R) % R), block((place(axis) - 2 * sign + R) % R)
+        for ref, k in ((three, 1), (three, -1), (two, sign)):
+            send(ref, ref, final, along(axis, k % R))
+
+    def q_block(kind, pair):
+        h = 4 * kind + pair
+        return lambda o: qbuf.at[h, o] if kind == 0 else qbuf.at[h, :, o]
+
     def q2_send(pair):
-        for k in ORDER:
-            for kind in KINDS:
-                h = 4 * kind + pair
-                ref = qbuf.at[h, z] if kind == 0 else qbuf.at[h, :, y]
-                send(ref, ref, slot(1, kind, pair), along(1 - kind, k))
+        for kind in KINDS:
+            spread(1 - kind, 1 - pair % 2 * 2, q_block(kind, pair), slot(1, kind, pair), slot(2, kind, pair))
+
+    def q2_relay(pair):
+        for kind in KINDS:
+            like = qbuf.at[4 * kind + pair, pl.ds(0, 2)]
+            relay(1 - kind, 1 - pair % 2 * 2, q_block(kind, pair), slot(1, kind, pair), slot(2, kind, pair), like)
 
     def q2_wait(pair):
         for kind in KINDS:
-            arrived(qbuf.at[4 * kind + pair, pl.ds(0, R - 1)], slot(1, kind, pair))
+            arrived(qbuf.at[4 * kind + pair, pl.ds(0, 5)], slot(2, kind, pair))
 
     lane = lax.broadcasted_iota(jnp.int32, (8, 128), 1)
     sub = lax.broadcasted_iota(jnp.int32, (8, 128), 0)
@@ -216,13 +233,19 @@
             snd1[kind, group, 2 * b, NH * 64 :, :] = even.astype(BF16)
             snd1[kind, group, 2 * b + 1, NH * 64 :, :] = odd.astype(BF16)
 
-    def r1_send(kind, group):
-        for k in ORDER:
-            to = (place(kind) + k) % R
-            send(snd1.at[kind, group, to], rcv1.at[kind, group, k - 1], slot(2, kind, group), along(kind, k))
+    def r1_rows(pair):
+        hh = pair % NH
+        return pl.ds(hh * 64, 64 if hh < NH - 1 else 64 + 16)
+
+    def r1_send(kind, pair):
+        group, rows = pair // NH, r1_rows(pair)
+        for k in ORDER:
+            src, dst = snd1.at[kind, group, (place(kind) + k) % R, rows], rcv1.at[kind, group, k - 1, rows]
+            send(src, dst, slot(3, kind, pair), along(kind, k))
 
     def r1_combine(kind, group):
-        arrived(rcv1.at[kind, group], slot(2, kind, group))
+        for pair in range(group * NH, (group + 1) * NH):
+            arrived(rcv1.at[kind, group, :, r1_rows(pair)], slot(3, kind, pair))
         own = snd1.at[kind, group, place(kind)]
         refs = [own] + [rcv1.at[kind, group, k] for k in range(R - 1)]
         logs = [unpack_stats(ref[NH * 64 :, :]) for ref in refs]
@@ -246,7 +269,7 @@
         axis = 1 - kind
         for k in ORDER:
             to = (place(axis) + k) % R
-            send(snd2.at[kind, group, to], rcv2.at[kind, group, k - 1], slot(3, kind, group), along(axis, k))
+            send(snd2.at[kind, group, to], rcv2.at[kind, group, k - 1], slot(4, kind, group), along(axis, k))
 
     def own_piece(kind, group):
         axis = 1 - kind
@@ -255,7 +278,7 @@
         return attn.at[kind, group, place(kind), me // PARTS, pl.ds(start, PIECE)]
 
     def r2_combine(kind, group):
-        arrived(rcv2.at[kind, group], slot(3, kind, group))
+        arrived(rcv2.at[kind, group], slot(4, kind, group))
         me = place(1 - kind)
         hh, part = me // PARTS, me % PARTS
         refs = [snd2.at[kind, group, me]] + [rcv2.at[kind, group, k] for k in range(R - 1)]
@@ -276,18 +299,21 @@
     def g1_send(kind, group):
         for k in ORDER:
             ref = own_piece(kind, group)
-            send(ref, ref, slot(4, kind, group), along(1 - kind, k))
+            send(ref, ref, slot(5, kind, group), along(1 - kind, k))
 
     def g1_wait(kind, group):
-        arrived(rcv2.at[kind, group, :, pl.ds(0, PIECE)], slot(4, kind, group))
+        arrived(rcv2.at[kind, group, :, pl.ds(0, PIECE)], slot(5, kind, group))
+
+    def g2_block(kind, group):
+        return lambda o: attn.at[kind, group, o]
 
     def g2_send(kind, group):
         ref = attn.at[kind, group, place(kind)]
         for k in ORDER:
-            send(ref, ref, slot(5, kind, group), along(kind, k))
+            send(ref, ref, slot(6, kind, group), along(kind, k))
 
     def g2_wait(kind, group):
-        arrived(attn.at[kind, group, pl.ds(0, R - 1)], slot(5, kind, group))
+        arrived(attn.at[kind, group, pl.ds(0, R - 1)], slot(6, kind, group))
 
     def project(kind, group):
         acc = None
@@ -307,7 +333,7 @@
                 total = term if total is None else total + term
         proj[...] = total
         snd3[...] = total.astype(BF16).reshape(R, 64, 128)
-        last = slot(6, 0, 0)
+        last = slot(8, 0, 0)
         for k in ORDER:
             to = (hd + k) % R
             send(snd3.at[to], rcv3.at[k - 1], last, {"head": to})
@@ -319,11 +345,15 @@
 
     steps = [(q1_send,), (prepare,), (q1_wait,)]
     steps += [(q2_send, pair) for pair in range(4)] + [(prepare_masks,)]
+    steps += [(q2_relay, pair) for pair in range(3)]
     for pair in range(4):
         steps += [(q2_wait, pair), (attend, pair)]
-        if pair % NH == NH - 1:
-            for kind in KINDS:
-                steps += [(statistics, kind, pair // NH), (r1_send, kind, pair // NH)]
+        for kind in KINDS:
+            if pair % NH == NH - 1:
+                steps += [(statistics, kind, pair // NH)]
+            steps += [(r1_send, kind, pair)]
+        if pair == 0:
+            steps += [(q2_relay, 3)]
     both = [(kind, group) for group in range(GROUPS) for kind in KINDS]
     for first, second in ((r1_combine, r2_send), (r2_combine, g1_send), (g1_wait, g2_send)):
         for args in both:
@@ -339,7 +369,7 @@
     keys, values = cache_keys[:, 0, :], cache_values[:, 0, :]
     local, width = keys.shape
     heads = vertical_blocks.shape[0]
-    slots = 6 * 2 * 4 + 1
+    slots = 8 * 2 * 4 + 1
     vmem, hbm = pl.BlockSpec(memory_space=pltpu.VMEM), pl.BlockSpec(memory_space=pltpu.HBM)
     return pl.pallas_call(
         kernel,

time: 72.1 us -> 70.6 us (0.979)
  Pallas kernels: 70.5 us -> 69 us
    pallas_call x1, Pallas kernels: 70.5 us -> 69 us  [body(): pl.pallas_call(kernel, out_shape=jax.ShapeDtypeStruct((64, 128), BF16), i...]
where the time goes in v3:
time: 70.6 us; the launch traced here: 70.3 us
  Pallas kernels  69 us (98%)
  local copies, waits for them, and re-layouts  1.32 us (2%)
    pallas_call x1, Pallas kernels, body(): pl.pallas_call(kernel, out_shape=jax.ShapeDtypeStruct((64, 128), BF16), i...  69 us

profile of v3, /device:TPU:1, one launch (start us, length us, event | category | flops | bytes accessed | tf_op | source)
XLA Modules:
  0.0 70.3 jit_solution(12051185348957354020)
XLA Ops:
  0.0 69.0 %shard_map.64 = bf16[64,128]{1,0:T(8,128)(2,1)} custom-call(bf16[8,1024]{1,0:T(8,128)(2,1)} %q_hbm.1, bf16[1024,128]{1,0:T(8,128)(2,1)} %bitcast.2, bf16[1024,128]{1,0:T(8,128)(2,1)} %bitcast.3, s32[8,8]{1,0:T(8,128)} %vert_hbm.1, s32[8,48]{1,0:T(8,128)} %slash_hbm.1, bf16[1024,128]{1,0:T(8,128)(2,1)} %w_hbm.1), custom_call_target="tpu_custom_call" | custom-call | tf_op jit(solution)/shard_map/pallas_call | solution.py:374
  69.0 1.3 %copy.8 = bf16[64,128]{1,0:T(8,128)(2,1)} copy(bf16[64,128]{1,0:T(8,128)(2,1)} %shard_map.64) | data formatting | bytes 32768

commit v4 on v3

--- a/solution.py
+++ b/solution.py
@@ -235,6 +235,8 @@
 
     def r1_rows(pair):
         hh = pair % NH
+        if pair < 4 - NH:
+            return pl.ds(0, ROWS1) if hh == NH - 1 else None
         return pl.ds(hh * 64, 64 if hh < NH - 1 else 64 + 16)
 
     def r1_send(kind, pair):
@@ -245,6 +247,8 @@
 
     def r1_combine(kind, group):
         for pair in range(group * NH, (group + 1) * NH):
+            if r1_rows(pair) is None:
+                continue
             arrived(rcv1.at[kind, group, :, r1_rows(pair)], slot(3, kind, pair))
         own = snd1.at[kind, group, place(kind)]
         refs = [own] + [rcv1.at[kind, group, k] for k in range(R - 1)]
@@ -351,7 +355,8 @@
         for kind in KINDS:
             if pair % NH == NH - 1:
                 steps += [(statistics, kind, pair // NH)]
-            steps += [(r1_send, kind, pair)]
+            if r1_rows(pair) is not None:
+                steps += [(r1_send, kind, pair)]
         if pair == 0:
             steps += [(q2_relay, 3)]
     both = [(kind, group) for group in range(GROUPS) for kind in KINDS]

time: 70.6 us -> 71.5 us (1.013)
  Pallas kernels: 69 us -> 69.8 us
    pallas_call x1, Pallas kernels: 69 us -> 69.8 us  [body(): pl.pallas_call(kernel, out_shape=jax.ShapeDtypeStruct((64, 128), BF16), i...]
where the time goes in v4:
time: 71.5 us; the launch traced here: 71.2 us
  Pallas kernels  69.8 us (98%)
  local copies, waits for them, and re-layouts  1.32 us (2%)
    pallas_call x1, Pallas kernels, body(): pl.pallas_call(kernel, out_shape=jax.ShapeDtypeStruct((64, 128), BF16), i...  69.8 us

profile of v4, /device:TPU:1, one launch (start us, length us, event | category | flops | bytes accessed | tf_op | source)
XLA Modules:
  0.0 71.2 jit_solution(6478827797957602586)
XLA Ops:
  0.0 69.8 %shard_map.64 = bf16[64,128]{1,0:T(8,128)(2,1)} custom-call(bf16[8,1024]{1,0:T(8,128)(2,1)} %q_hbm.1, bf16[1024,128]{1,0:T(8,128)(2,1)} %bitcast.2, bf16[1024,128]{1,0:T(8,128)(2,1)} %bitcast.3, s32[8,8]{1,0:T(8,128)} %vert_hbm.1, s32[8,48]{1,0:T(8,128)} %slash_hbm.1, bf16[1024,128]{1,0:T(8,128)(2,1)} %w_hbm.1), custom_call_target="tpu_custom_call" | custom-call | tf_op jit(solution)/shard_map/pallas_call | solution.py:379
  69.8 1.3 %copy.8 = bf16[64,128]{1,0:T(8,128)(2,1)} copy(bf16[64,128]{1,0:T(8,128)(2,1)} %shard_map.64) | data formatting | bytes 32768
